TPU v7x, 128 devices: a whole 4x4x4 slice. The times are simulated.
128 devices in a mesh: tensor: 4 (over y), context: 4 (over x_hi, core), dp: 8 (over z, x_lo).
Axes of the slice: x: 4 (x_hi: 2, x_lo: 2; x = x_hi * 2 + x_lo), y: 4, z: 4, core: 2. Of those that a mesh axis runs over, the one named last changes fastest.
Arguments:
- tokens: bfloat16 [16384, 4096], P(('tensor', 'context', 'dp')), may hold values from -6 to 6
- gates: float32 [16384, 2], P(('tensor', 'context', 'dp')), may hold values from 0.1 to 0.9
- routes: int32 [16384, 2], P(('tensor', 'context', 'dp')), may hold values from 0 to 15, all different within a row; in each aligned block of 128 rows (0 to 127, 128 to 255, ...) at most 24 rows name the same one
- w_in: bfloat16 [16, 4096, 1536], P(('tensor', 'context')), may hold values from -0.09375 to 0.09375
- w_out: bfloat16 [16, 768, 4096], P(('tensor', 'context')), may hold values from -0.21875 to 0.21875
- cotangent: bfloat16 [16384, 4096], P(('tensor', 'context', 'dp')), may hold values from -6 to 6
Outputs:
- mixed: bfloat16 [16384, 4096], P(('tensor', 'context', 'dp'))
- grad_tokens: bfloat16 [16384, 4096], P(('tensor', 'context', 'dp'))
- grad_gates: float32 [16384, 2], P(('tensor', 'context', 'dp'))
- grad_w_in: bfloat16 [65536, 1536], P(('tensor', 'context', 'dp'))
- grad_w_out: bfloat16 [12288, 4096], P(('tensor', 'context', 'dp'))
Inputs may be any that keep to these rules, and one draw needn't show every extreme that they name: `routes`: each row names 2 different experts; among the 128 rows of one device (aligned blocks) no expert is named more than 24 times, a bound that some block reaches.
All inputs are finite; a program needn't handle non-finite values.
Results may differ from a plain program's by a relative error of at most 0.019.
Values may be sent and summed in bfloat16 or wider, within the bound.
A program may use at most 128 MiB of HBM per device.

v0:
```python
import jax
import jax.numpy as jnp
from jax import lax
from jax.sharding import PartitionSpec as P


def trade_rows(buffer):
    return lax.all_to_all(buffer, ("tensor", "context"), split_axis=0, concat_axis=0, tiled=True)


def expert_forward(inputs_flat, weight_in, weight_out):
    hidden_units = weight_out.shape[0]
    gate_up = jnp.dot(inputs_flat, weight_in, preferred_element_type=jnp.float32)
    gate_part = gate_up[:, :hidden_units]
    up_part = gate_up[:, hidden_units:]
    sigmoid_gate = jax.nn.sigmoid(gate_part)
    hidden = (gate_part * sigmoid_gate * up_part).astype(jnp.bfloat16)
    outputs = jnp.dot(hidden, weight_out, preferred_element_type=jnp.float32).astype(jnp.bfloat16)
    return (gate_part, up_part, sigmoid_gate, hidden, outputs)


def expert_backward(grads_flat, gate_part, up_part, sigmoid_gate, weight_out):
    grad_hidden = lax.dot_general(
        grads_flat, weight_out, (((1,), (1,)), ((), ())), preferred_element_type=jnp.float32
    )
    grad_gate = grad_hidden * up_part * sigmoid_gate * (1.0 + gate_part * (1.0 - sigmoid_gate))
    grad_up = grad_hidden * gate_part * sigmoid_gate
    return jnp.concatenate([grad_gate, grad_up], axis=1).astype(jnp.bfloat16)


def shards(tokens, gates, routes, w_in, w_out, cotangent):
    experts = lax.axis_size(("tensor", "context"))
    tok_count, top_count = routes.shape
    model_width = tokens.shape[1]
    capacity = tok_count * top_count // experts + tok_count * top_count // (2 * experts)
    total_routes = tok_count * top_count
    route_ids = routes.reshape(-1)
    matches = (route_ids[:, None] == jnp.arange(experts, dtype=jnp.int32)[None, :]).astype(
        jnp.int32
    )
    slot_index = jnp.sum((jnp.cumsum(matches, axis=0) - matches) * matches, axis=1)
    positions = route_ids * capacity + slot_index
    empty = jnp.full((experts * capacity,), total_routes, jnp.int32)
    slot_table = empty.at[positions].set(jnp.arange(total_routes, dtype=jnp.int32))
    occupied = slot_table < total_routes
    safe_routes = jnp.minimum(slot_table, total_routes - 1)
    token_rows = safe_routes // top_count
    route_gate = jnp.where(occupied, gates.reshape(-1)[safe_routes], jnp.zeros((), gates.dtype))
    send_inputs = jnp.where(occupied[:, None], tokens[token_rows], jnp.zeros((), tokens.dtype))
    send_inputs = send_inputs.reshape(experts, capacity, model_width)
    send_grads = (route_gate[:, None] * cotangent[token_rows].astype(jnp.float32)).astype(
        jnp.bfloat16
    )
    send_grads = send_grads.reshape(experts, capacity, model_width)
    weight_in = w_in[0]
    weight_out = w_out[0]
    arrived = trade_rows(jnp.concatenate([send_inputs, send_grads], axis=1))
    inputs_here = arrived[:, :capacity]
    grads_here = arrived[:, capacity:]
    inputs_flat = inputs_here.reshape(-1, model_width)
    gate_part, up_part, sigmoid_gate, hidden, outputs = expert_forward(
        inputs_flat, weight_in, weight_out
    )
    grads_flat = grads_here.reshape(-1, model_width)
    grad_gate_up = expert_backward(grads_flat, gate_part, up_part, sigmoid_gate, weight_out)
    route_dx = lax.dot_general(
        grad_gate_up, weight_in, (((1,), (1,)), ((), ())), preferred_element_type=jnp.float32
    ).astype(jnp.bfloat16)
    stacked = jnp.concatenate(
        [
            outputs.reshape(experts, capacity, model_width),
            route_dx.reshape(experts, capacity, model_width),
        ],
        axis=1,
    )
    returned = trade_rows(stacked)
    out_back = returned[:, :capacity]
    dx_back = returned[:, capacity:]
    piece = hidden
    grad_out = lax.psum_scatter(
        lax.dot_general(
            piece, grads_flat, (((0,), (0,)), ((), ())), preferred_element_type=jnp.float32
        ).astype(jnp.bfloat16),
        "dp",
        scatter_dimension=0,
        tiled=True,
    )
    piece = inputs_flat
    grad_in = lax.psum_scatter(
        lax.dot_general(
            piece, grad_gate_up, (((0,), (0,)), ((), ())), preferred_element_type=jnp.float32
        ).astype(jnp.bfloat16),
        "dp",
        scatter_dimension=0,
        tiled=True,
    )
    out_routes = (
        out_back.reshape(-1, model_width)[positions]
        .reshape(tok_count, top_count, model_width)
        .astype(jnp.float32)
    )
    mixed_out = jnp.sum(gates[:, :, None] * out_routes, axis=1).astype(jnp.bfloat16)
    grad_gates = jnp.sum(cotangent[:, None, :].astype(jnp.float32) * out_routes, axis=2)
    dx_routes = (
        dx_back.reshape(-1, model_width)[positions]
        .reshape(tok_count, top_count, model_width)
        .astype(jnp.float32)
    )
    grad_tokens = jnp.sum(dx_routes, axis=1).astype(jnp.bfloat16)
    return (mixed_out, grad_tokens, grad_gates, grad_in, grad_out)


def solution(mesh):
    placed = (
        P(("tensor", "context", "dp"), None),
        P(("tensor", "context", "dp"), None),
        P(("tensor", "context", "dp"), None),
        P(("tensor", "context"), None, None),
        P(("tensor", "context"), None, None),
        P(("tensor", "context", "dp"), None),
    )
    return jax.shard_map(
        shards,
        mesh=mesh,
        in_specs=placed,
        out_specs=(
            P(("tensor", "context", "dp"), None),
            P(("tensor", "context", "dp"), None),
            P(("tensor", "context", "dp"), None),
            P(("tensor", "context", "dp"), None),
            P(("tensor", "context", "dp"), None),
        ),
        check_vma=False,
    )
```

profile of v0, /device:TPU:1, one launch (start us, length us, event | category | flops | bytes accessed | tf_op | source)
XLA Modules:
  0.0 586.9 jit_solution(5935086358571034721)
XLA Ops:
  12.7 2.8 gather_fusion.1
  15.7 4.0 gather_fusion.2
  19.8 4.1 gather_fusion
  23.8 3.0 fusion.4
  26.9 1.9 broadcast_select_fusion
  28.8 2.7 pad_maximum_fusion
  31.5 81.3 %all_to_all.10 = bf16[16,48,4096]{2,1,0:T(8,128)(2,1)S(1)} all-to-all(bf16[16,48,4096]{2,1,0:T(8,128)(2,1)S(1)} %pad_maximum_fusion), channel_id=1, replica_groups=mesh['tensor'=4,'context'=4,'dp'=8] {'tensor','context'}, dimensions={0} | all-to-all | bytes 12582912 | tf_op jit(solution)/shard_map/all_to_all | solution.py:8
  113.7 9.5 %fusion.2 = f32[384,1536]{1,0:T(8,128)S(1)} fusion(bf16[384,4096]{1,0:T(8,128)(2,1)S(1)} %bitcast.57, bf16[1,4096,1536]{2,1,0:T(8,128)(2,1)} %param.9), kind=kOutput, calls=%fused_computation.9 | convolution fusion | flops 4831838208 | bytes 18087936 | tf_op jit(solution)/shard_map/dot_general | solution.py:13
  123.3 3.8 multiply_convert_fusion.1
  127.1 5.4 convolution_convert_fusion.1
  132.8 11.2 %convolution_convert_fusion = bf16[4096,1536]{1,0:T(8,128)(2,1)} fusion(bf16[384,4096]{1,0:T(8,128)(2,1)} %bitcast.58, bf16[384,768]{1,0:T(8,128)(2,1)} %get-tuple-element.19, bf16[384,768]{1,0:T(8,128)(2,1)S(1)} %get-tuple-element.18), kind=kOutput, calls=%fused_computation.6 | convolution fusion | flops 4840488960 | bytes 16908288 | tf_op jit(solution)/shard_map/dot_general | solution.py:90
  144.0 5.8 fusion.12
  149.7 17.2 %fusion.9 = bf16[384,4096]{1,0:T(8,128)(2,1)S(1)} fusion(bf16[1,4096,1536]{2,1,0:T(8,128)(2,1)} %param.9, bf16[384,768]{1,0:T(8,128)(2,1)S(1)} %copy-done.6, bf16[384,768]{1,0:T(8,128)(2,1)S(1)} %get-tuple-element.18), kind=kOutput, calls=%fused_computation.20 | convolution fusion | flops 4835770368 | bytes 16908288 | tf_op jit(solution)/shard_map/dot_general | solution.py:66
  166.9 3.5 pad_maximum_fusion.1
  170.5 5.5 all-to-all-start.1
  177.5 140.0 %all-to-all-done.1 = bf16[16,48,4096]{2,1,0:T(8,128)(2,1)} async-done(((bf16[16,48,4096]{2,1,0:T(8,128)(2,1)}), bf16[16,48,4096]{2,1,0:T(8,128)(2,1)}, u32[]{:S(2)}, u32[]{:S(2)}) %all-to-all-start.1) | async-done | bytes 6291488 | tf_op jit(solution)/shard_map/all_to_all | solution.py:8
  317.5 5.3 fusion.25
  322.8 7.7 %gather_fusion.4 = bf16[256,4096]{1,0:T(8,128)(2,1)} fusion(bf16[384,4096]{1,0:T(8,128)(2,1)} %bitcast.54, s32[1024]{0:T(1024)S(1)} %pad_clamp_fusion), kind=kCustom, calls=%fused_computation.4 | custom fusion | bytes 4195328 | tf_op jit(solution)/shard_map/gather | solution.py:105
  330.5 4.4 reshape.122
  334.9 3.2 gather_fusion.3
  338.1 5.9 %reshape.124 = f32[128,2,4096]{2,1,0:T(2,128)} reshape(bf16[256,4096]{1,0:T(8,128)(2,1)} %gather_fusion.3) | data formatting | bytes 6291456 | tf_op jit(solution)/shard_map/convert_element_type | solution.py:100
  344.0 10.5 %multiply_reduce_fusion = (f32[128,2]{1,0:T(8,128)S(1)}, bf16[128,4096]{1,0:T(8,128)(2,1)}) fusion(f32[128,2,4096]{2,1,0:T(2,128)} %reshape.124, f32[128,4096]{1,0:T(8,128)S(1)} %copy-done.4, f32[128,2]{1,0:T(8,128)S(1)} %copy.18), kind=kLoop, calls=%fused_computation.22 | loop fusion | flops 3669760 | bytes 7342080 | tf_op jit(solution)/shard_map/reduce_sum | solution.py:103
  355.1 7.7 %reduce_sum.44 = bf16[128,4096]{1,0:T(8,128)(2,1)} reduce(bf16[128,2,4096]{2,1,0:T(2,128)(2,1)} %reshape.122, bf16[]{:T(256)} %constant.35.clone.1), dimensions={1}, to_apply=%region_5.6 | reduce | flops 524288 | bytes 3145730 | tf_op jit(solution)/shard_map/reduce_sum | solution.py:109
  362.8 217.3 %reduce-scatter.3.cloned.1.call-done = bf16[512,1536]{1,0:T(8,128)(2,1)} async-done(((bf16[4096,1536]{1,0:T(8,128)(2,1)}), bf16[512,1536]{1,0:T(8,128)(2,1)}) %reduce-scatter.3.cloned.1.call-update) | async-done | bytes 1572880 | tf_op jit(solution)/shard_map/reduce_scatter | solution.py:89
  (50 shorter events, 8.9 us)
Async XLA Ops:
  7.2 12.6 %copy-start = (bf16[128,4096]{1,0:T(8,128)(2,1)S(1)}, bf16[128,4096]{1,0:T(8,128)(2,1)}, u32[]{:S(2)}) copy-start(bf16[128,4096]{1,0:T(8,128)(2,1)} %param.6) | copy-start | bytes 3145732
  7.2 8.5 %copy-start.2 = (bf16[128,4096]{1,0:T(8,128)(2,1)S(1)}, bf16[128,4096]{1,0:T(8,128)(2,1)}, u32[]{:S(2)}) copy-start(bf16[128,4096]{1,0:T(8,128)(2,1)} %param.11) | copy-start | bytes 3145732
  7.2 355.6 %reduce-scatter.5.cloned.1.call-start = ((), (), s32[]{:S(2)}) async-start(), calls=%async_computation.5 | async-start | bytes 7077888 | tf_op jit(solution)/shard_map/reduce_scatter | solution.py:80
  23.8 3.1 copy-start.3
  112.9 10.4 %slice-start = ((s8[6291456]{0:T(1024)(128)(4,1)}), s8[4194304]{0:T(1024)(128)(4,1)S(1)}, s32[]{:S(2)}) async-start(s8[6291456]{0:T(1024)(128)(4,1)} %bitcast.66), calls=%async_computation.6 | async-start | bytes 8388608
  113.6 9.6 %copy-start.5 = (bf16[16,24,4096]{2,1,0:T(8,128)(2,1)}, bf16[16,24,4096]{2,1,0:T(8,128)(2,1)S(1)}, u32[]{:S(2)}) copy-start(bf16[16,24,4096]{2,1,0:T(8,128)(2,1)S(1)} %get-tuple-element.16) | copy-start | bytes 9437188
  113.7 9.6 %slice-start.1 = ((s8[6291456]{0:T(1024)(128)(4,1)}), s8[2097152]{0:T(1024)(128)(4,1)S(1)}, s32[]{:S(2)}) async-start(s8[6291456]{0:T(1024)(128)(4,1)} %bitcast.66), calls=%async_computation.7 | async-start | bytes 4194304
  132.5 447.6 %reduce-scatter.3.cloned.1.call-start = ((), (), s32[]{:S(2)}) async-start(), calls=%async_computation.4 | async-start | bytes 14155776 | tf_op jit(solution)/shard_map/reduce_scatter | solution.py:89
  143.9 5.8 copy-start.6
  170.5 147.0 %all-to-all-start.1 = ((bf16[16,48,4096]{2,1,0:T(8,128)(2,1)}), bf16[16,48,4096]{2,1,0:T(8,128)(2,1)}, u32[]{:S(2)}, u32[]{:S(2)}) async-start(bf16[16,48,4096]{2,1,0:T(8,128)(2,1)} %pad_maximum_fusion.1), calls=%async_computation.1 | async-start | bytes 12582912 | tf_op jit(solution)/shard_map/all_to_all | solution.py:8
  338.1 5.9 %copy-start.4 = (f32[128,4096]{1,0:T(8,128)S(1)}, f32[128,4096]{1,0:T(8,128)}, u32[]{:S(2)}) copy-start(f32[128,4096]{1,0:T(8,128)} %convert_element_type.64) | copy-start | bytes 6291460
  344.0 236.1 %copy-start.1 = (bf16[128,4096]{1,0:T(8,128)(2,1)S(1)}, bf16[128,4096]{1,0:T(8,128)(2,1)}, u32[]{:S(2)}) copy-start(bf16[128,4096]{1,0:T(8,128)(2,1)} %param.6) | copy-start | bytes 3145732
Sparse Core Ops, SparseCore 0:
  132.6 195.5 reduce-scatter.4
  331.2 248.8 reduce-scatter.2
where the time goes:
time: 587 us
  waiting for transfers between devices  357 us (61%)
  blocking collectives  81.3 us (14%)
  matrix products  52.9 us (9%)
  local copies, waits for them, and re-layouts  42.9 us (7%)
  other arithmetic  32.5 us (6%)
  between operations  14.3 us (2%)
    reduce_scatter x1, waiting for transfers between devices, shards(): lax.psum_scatter(lax.dot_general(piece, grad_gate_up, (((0,), (0,)), ((),...  217 us
    all_to_all x1, waiting for transfers between devices, trade_rows(): lax.all_to_all(buffer, ('tensor', 'context'), split_axis=0, concat_axis=0...  140 us
    all_to_all x1, blocking collectives, trade_rows(): lax.all_to_all(buffer, ('tensor', 'context'), split_axis=0, concat_axis=0...  81.3 us
    dot_general x1, matrix products, shards(): lax.dot_general(grad_gate_up, weight_in, (((1,), (1,)), ((), ())), prefer...  17.2 us
  transfers between devices with their start and end apart: 3, of which 2 were waited for; matrix products, arithmetic and copies ran while one was open for 14% of the time, Pallas kernels for 0%

commit v1 on v0

v1 whole, which is shorter than its diff:
```python
import jax
import jax.numpy as jnp
from jax import lax
from jax.experimental import pallas as pl
from jax.experimental.pallas import tpu as pltpu
from jax.sharding import PartitionSpec as P

MESH = pl.DeviceIdType.MESH
BF = jnp.bfloat16
F32 = jnp.float32

D = 4096
F = 768
CAP = 24
SLOTS = 16
ROWS = SLOTS * CAP
TOK = 128
OWN = 12
QD = D // 4
HD = D // 2


def dot(a, b):
    return jnp.dot(a, b, preferred_element_type=F32)


def dot_nt(a, b):
    return lax.dot_general(a, b, (((1,), (1,)), ((), ())), preferred_element_type=F32)


def dot_tn(a, b):
    return lax.dot_general(a, b, (((0,), (0,)), ((), ())), preferred_element_type=F32)


def split_rows(block):
    wide = block.astype(F32)
    n = wide.shape[-1]
    first = wide[:, :CAP, :].reshape(ROWS, n).astype(BF)
    last = wide[:, CAP:, :].reshape(ROWS, n).astype(BF)
    return first, last


def join_rows(first, last):
    n = first.shape[-1]
    s = first.shape[0] // CAP
    return jnp.concatenate([first.reshape(s, CAP, n), last.reshape(s, CAP, n)], axis=1).astype(BF)


def kernel(
    tok_hbm, cot_hbm, routes_ref, gates_ref, win_hbm, wout_hbm,
    mixed_ref, gtok_ref, ggate_ref, gin_ref, gout_ref, ro_hbm, rdx_hbm,
    send, rx, xdz, win, wout, fs, agb, go, gs_in, gr_in, gs_out, gr_out, gt_s, gt_r,
    sel, smat, gcol, stmat, gmat, sval, sret,
    d_ss, d_rs, z_ss, z_rs, a_ss, a_rs, o_ss, o_rs, x_ss, x_rs, s_ss, s_rs, e_ss, e_rs, t_ss, t_rs, loc,
):
    y = lax.axis_index("tensor")
    c = lax.axis_index("context")
    d = lax.axis_index("dp")
    z = d // 2
    xl = d % 2

    def to_expert(i):
        j, m = i // 4, i % 4
        return ((y + 1 + j) % 4, (c + m) % 4, d)

    def to_source(i):
        j, m = i // 4, i % 4
        return ((y + 3 - j) % 4, (c + 4 - m) % 4, d)

    def z_peer(k):
        return (y, c, ((z + k) % 4) * 2 + xl)

    pair = (y, c, z * 2 + (1 - xl))

    def remote(src, dst, ss, rs, dev):
        return pltpu.make_async_remote_copy(
            src_ref=src, dst_ref=dst, send_sem=ss, recv_sem=rs, device_id=dev, device_id_type=MESH
        )

    ld_tok = pltpu.make_async_copy(tok_hbm, mixed_ref, loc.at[0])
    ld_cot = pltpu.make_async_copy(cot_hbm, gtok_ref, loc.at[1])
    ld_win = pltpu.make_async_copy(win_hbm.at[0], win, loc.at[2])
    ld_wout = pltpu.make_async_copy(wout_hbm.at[0], wout, loc.at[3])
    ld_tok.start()
    ld_cot.start()

    bar = pltpu.get_barrier_semaphore()
    for i in range(SLOTS):
        if i != OWN:
            pl.semaphore_signal(bar, inc=1, device_id=to_expert(i), device_id_type=MESH)
    for k in (1, 2, 3):
        pl.semaphore_signal(bar, inc=1, device_id=z_peer(k), device_id_type=MESH)
    pl.semaphore_signal(bar, inc=1, device_id=pair, device_id_type=MESH)

    r0 = routes_ref[0:1, :]
    r1 = routes_ref[1:2, :]
    ids = lax.broadcasted_iota(jnp.int32, (SLOTS, TOK), 0)
    match = jnp.where((ids == r0) | (ids == r1), 1.0, 0.0).astype(BF)
    before = jnp.where(
        lax.broadcasted_iota(jnp.int32, (TOK, TOK), 0) < lax.broadcasted_iota(jnp.int32, (TOK, TOK), 1),
        1.0, 0.0,
    ).astype(BF)
    rank = dot(match, before).astype(BF)
    row = lax.broadcasted_iota(jnp.int32, (ROWS, TOK), 0)
    slot = (row * 683) >> 14
    place = (row - slot * CAP).astype(F32)
    expert = ((y + 1 + (slot >> 2)) & 3) * 4 + ((c + (slot & 3)) & 3)
    pick = jnp.where(
        expert[:, :SLOTS] == lax.broadcasted_iota(jnp.int32, (ROWS, SLOTS), 1), 1.0, 0.0
    ).astype(BF)
    here = dot(pick, rank) == place
    s0 = jnp.where((expert == r0) & here, 1.0, 0.0)
    s1 = jnp.where((expert == r1) & here, 1.0, 0.0)
    sel[0] = s0
    sel[1] = s1
    both = s0 + s1
    smat[...] = both.astype(BF)
    gsel = s0 * gates_ref[0:1, :] + s1 * gates_ref[1:2, :]
    gcol[...] = jnp.broadcast_to(jnp.sum(gsel, axis=1, keepdims=True), (ROWS, TOK))
    stmat[...] = both.T.astype(BF)
    gt = gsel.T
    ghi = gt.astype(BF)
    gmat[0] = ghi
    gmat[1] = (gt - ghi.astype(F32)).astype(BF)

    ld_tok.wait()
    ld_cot.wait()
    ld_win.start()
    ld_wout.start()
    pl.semaphore_wait(bar, 19)

    d_cp = {}
    for j in range(4):
        g0 = j * 4 * CAP

        @pl.loop(0, 4)
        def _(n):
            cs = pl.ds(pl.multiple_of(n * 1024, 1024), 1024)
            sm = smat[g0:g0 + 4 * CAP, :]
            a = dot(sm, mixed_ref[:, cs])
            b = dot(sm, gtok_ref[:, cs]) * gcol[g0:g0 + 4 * CAP, 0:1]
            send[4 * j:4 * j + 4, :, cs] = join_rows(a, b)

        for m in range(4):
            i = 4 * j + m
            if i == OWN:
                d_cp[i] = pltpu.make_async_copy(send.at[i], rx.at[i], loc.at[4])
            else:
                d_cp[i] = remote(send.at[i], rx.at[i], d_ss.at[i], d_rs.at[i], to_expert(i))
            d_cp[i].start()

    z_cp = []
    for j in (3, 0, 2, 1):
        for m in range(4):
            i = 4 * j + m
            if i == OWN:
                d_cp[i].wait()
            else:
                d_cp[i].wait_recv()
        for k in (1, 2, 3):
            n = j * 3 + k - 1
            cols = pl.ds(pl.multiple_of(((z + k) % 4) * QD, QD), QD)
            cp = remote(
                rx.at[4 * j:4 * j + 4, :, cols], xdz.at[k - 1, 4 * j:4 * j + 4],
                z_ss.at[n], z_rs.at[n], z_peer(k),
            )
            cp.start()
            z_cp.append(cp)

    ld_win.wait()
    ld_wout.wait()
    fs[...] = jnp.zeros_like(fs)

    @pl.loop(0, 8)
    def _(n):
        ks = pl.ds(pl.multiple_of(n * 512, 512), 512)
        xk, dk = split_rows(rx[:, :, ks])
        fs[0:ROWS, :] += dot(xk, win[ks, 0:F])
        fs[ROWS:2 * ROWS, :] += dot(xk, win[ks, F:2 * F])
        fs[2 * ROWS:3 * ROWS, :] += dot_nt(dk, wout[:, ks])

    @pl.loop(0, 8)
    def _(n):
        r = pl.multiple_of(n * 48, 48)
        g = fs[pl.ds(r, 48), :]
        u = fs[pl.ds(r + ROWS, 48), :]
        dh = fs[pl.ds(r + 2 * ROWS, 48), :]
        s = jax.nn.sigmoid(g)
        h = (g * s * u).astype(BF)
        rs = pl.ds(r, 48)
        agb[2, 3, rs, :] = h
        agb[0, 3, rs, :] = (dh * u * s * (1.0 + g * (1.0 - s))).astype(BF)
        agb[1, 3, rs, :] = (dh * g * s).astype(BF)
        sval[rs, :] = jnp.broadcast_to(jnp.sum(h.astype(F32) * dh, axis=1, keepdims=True), (48, TOK))

    a_cp = {}
    for p in (2, 0, 1):
        for k in (1, 2, 3):
            n = p * 3 + k - 1
            a_cp[p, k] = remote(agb.at[p, 3], agb.at[p, k - 1], a_ss.at[n], a_rs.at[n], z_peer(k))
            a_cp[p, k].start()

    for i in range(SLOTS):
        if i != OWN:
            d_cp[i].wait_send()

    @pl.loop(0, 4)
    def _(n):
        c0 = pl.multiple_of(n * 512, 512)
        h = agb[2, 3]
        a = dot(h, wout[:, pl.ds(c0, 512)])
        b = dot(h, wout[:, pl.ds(c0 + HD, 512)])
        send[:, :, pl.ds(c0, 512)] = join_rows(a, b)

    o_cp, x_cp, s_cp = {}, {}, {}
    for i in range(SLOTS):
        rows = pl.ds(i * CAP, CAP)
        if i == OWN:
            s_cp[i] = pltpu.make_async_copy(sval.at[rows], sret.at[rows], loc.at[5])
        else:
            o_cp[i] = remote(send.at[i, :, 0:HD], ro_hbm.at[i], o_ss.at[i], o_rs.at[i], to_source(i))
            o_cp[i].start()
            s_cp[i] = remote(sval.at[rows], sret.at[rows], s_ss.at[i], s_rs.at[i], to_source(i))
        s_cp[i].start()

    @pl.loop(0, 4)
    def _(n):
        c0 = pl.multiple_of(n * 512, 512)
        dg = agb[0, 3]
        du = agb[1, 3]
        lo = pl.ds(c0, 512)
        hi = pl.ds(c0 + HD, 512)
        a = dot_nt(dg, win[lo, 0:F]) + dot_nt(du, win[lo, F:2 * F])
        b = dot_nt(dg, win[hi, 0:F]) + dot_nt(du, win[hi, F:2 * F])
        send[:, :, pl.ds(c0 + HD, 512)] = join_rows(a, b)

    for i in range(SLOTS):
        if i != OWN:
            x_cp[i] = remote(send.at[i, :, HD:D], rdx_hbm.at[i], x_ss.at[i], x_rs.at[i], to_source(i))
            x_cp[i].start()

    for cp in z_cp:
        cp.wait()
    own0 = z * QD
    e_cp = []
    for k in (1, 2, 3):
        a_cp[2, k].wait()

    @pl.loop(0, 2)
    def _(n):
        n0 = pl.multiple_of(n * 512, 512)
        acc = None
        for s in range(4):
            if s < 3:
                blk = xdz[s, :, :, pl.ds(n0, 512)]
            else:
                blk = rx[:, :, pl.ds(pl.multiple_of(own0 + n0, 512), 512)]
            _, dk = split_rows(blk)
            t = dot_tn(agb[2, s], dk)
            acc = t if acc is None else acc + t
        go[:, pl.ds(n0, 512)] = acc

    for q in range(4):
        r = pl.multiple_of(q * 192 + (1 - xl) * 96, 96)
        gs_out[q] = go[pl.ds(r, 96), :].astype(BF)
    cp = remote(gs_out, gr_out, e_ss.at[2], e_rs.at[2], pair)
    cp.start()
    e_cp.append(cp)

    for p in range(2):
        for k in (1, 2, 3):
            a_cp[p, k].wait()

        def half(side, store):
            @pl.loop(0, 2)
            def _(n):
                n0 = pl.multiple_of(n * 256, 256)
                acc = None
                for s in range(4):
                    off = pl.multiple_of(side * 512 + n0, 256)
                    if s < 3:
                        blk = xdz[s, :, :, pl.ds(off, 256)]
                    else:
                        blk = rx[:, :, pl.ds(pl.multiple_of(own0 + off, 256), 256)]
                    xk, _ = split_rows(blk)
                    t = dot_tn(xk, agb[p, s])
                    acc = t if acc is None else acc + t
                store(n0, acc)

        def store_send(n0, acc):
            gs_in[p, pl.ds(n0, 256), :] = acc.astype(BF)

        def store_own(n0, acc):
            fs[pl.ds(p * 512 + n0, 256), :] = acc

        half(1 - xl, store_send)
        cp = remote(gs_in.at[p], gr_in.at[p], e_ss.at[p], e_rs.at[p], pair)
        cp.start()
        e_cp.append(cp)
        half(xl, store_own)

    e_cp[0].wait()
    for q in range(4):
        r = pl.multiple_of(q * 192 + xl * 96, 96)
        gt_s[q] = (go[pl.ds(r, 96), :] + gr_out[q].astype(F32)).astype(BF)
    t_cp = []
    for k in (1, 2, 3):
        cp = remote(gt_s.at[(z + k) % 4], gt_r.at[k - 1], t_ss.at[k - 1], t_rs.at[k - 1], z_peer(k))
        cp.start()
        t_cp.append(cp)
    gout_ref[:, pl.ds(pl.multiple_of(own0, QD), QD)] = gt_s[z]

    for i in range(SLOTS):
        if i != OWN:
            s_cp[i].wait()
            o_cp[i].wait()
        else:
            s_cp[i].wait()
    for k in range(2):
        ggate_ref[k:k + 1, :] = (
            jnp.sum(sel[k] * sret[...], axis=0, keepdims=True) / gates_ref[k:k + 1, :]
        )
    back = []
    for i in range(SLOTS):
        src = send.at[i, :, 0:HD] if i == OWN else ro_hbm.at[i]
        back.append(pltpu.make_async_copy(src, rx.at[i, :, 0:HD], loc.at[6 + i]))
        back[-1].start()
    for cp in back:
        cp.wait()

    @pl.loop(0, 4)
    def _(n):
        c0 = pl.multiple_of(n * 512, 512)
        a, b = split_rows(rx[:, :, pl.ds(c0, 512)])
        mixed_ref[:, pl.ds(c0, 512)] = (dot(gmat[0], a) + dot(gmat[1], a)).astype(BF)
        mixed_ref[:, pl.ds(c0 + HD, 512)] = (dot(gmat[0], b) + dot(gmat[1], b)).astype(BF)

    for i in range(SLOTS):
        if i != OWN:
            x_cp[i].wait()
    back = []
    for i in range(SLOTS):
        src = send.at[i, :, HD:D] if i == OWN else rdx_hbm.at[i]
        back.append(pltpu.make_async_copy(src, rx.at[i, :, HD:D], loc.at[6 + i]))
        back[-1].start()
    for cp in back:
        cp.wait()

    @pl.loop(0, 4)
    def _(n):
        c0 = pl.multiple_of(n * 512, 512)
        a, b = split_rows(rx[:, :, pl.ds(c0 + HD, 512)])
        gtok_ref[:, pl.ds(c0, 512)] = dot(stmat[...], a).astype(BF)
        gtok_ref[:, pl.ds(c0 + HD, 512)] = dot(stmat[...], b).astype(BF)

    for p in range(2):
        e_cp[1 + p].wait()
        gin_ref[:, p * F:(p + 1) * F] = (
            fs[p * 512:(p + 1) * 512, :] + gr_in[p].astype(F32)
        ).astype(BF)

    for k in (1, 2, 3):
        t_cp[k - 1].wait()
        col = pl.multiple_of(((z + 4 - k) % 4) * QD, QD)
        gout_ref[:, pl.ds(col, QD)] = gt_r[k - 1]


def shards(tokens, gates, routes, w_in, w_out, cotangent):
    hbm = pl.BlockSpec(memory_space=pl.ANY)
    vm = pl.BlockSpec(memory_space=pltpu.VMEM)
    dma = pltpu.SemaphoreType.DMA
    outs = pl.pallas_call(
        kernel,
        name="experts",
        out_shape=(
            jax.ShapeDtypeStruct((TOK, D), BF),
            jax.ShapeDtypeStruct((TOK, D), BF),
            jax.ShapeDtypeStruct((2, TOK), F32),
            jax.ShapeDtypeStruct((512, 2 * F), BF),
            jax.ShapeDtypeStruct((96, D), BF),
            jax.ShapeDtypeStruct((SLOTS, 48, HD), BF),
            jax.ShapeDtypeStruct((SLOTS, 48, HD), BF),
        ),
        in_specs=[hbm, hbm, vm, vm, hbm, hbm],
        out_specs=(vm, vm, vm, vm, vm, hbm, hbm),
        scratch_shapes=[
            pltpu.VMEM((SLOTS, 48, D), BF),
            pltpu.VMEM((SLOTS, 48, D), BF),
            pltpu.VMEM((3, SLOTS, 48, QD), BF),
            pltpu.VMEM((D, 2 * F), BF),
            pltpu.VMEM((F, D), BF),
            pltpu.VMEM((3 * ROWS, F), F32),
            pltpu.VMEM((3, 4, ROWS, F), BF),
            pltpu.VMEM((F, QD), F32),
            pltpu.VMEM((2, 512, F), BF),
            pltpu.VMEM((2, 512, F), BF),
            pltpu.VMEM((4, 96, QD), BF),
            pltpu.VMEM((4, 96, QD), BF),
            pltpu.VMEM((4, 96, QD), BF),
            pltpu.VMEM((3, 96, QD), BF),
            pltpu.VMEM((2, ROWS, TOK), F32),
            pltpu.VMEM((ROWS, TOK), BF),
            pltpu.VMEM((ROWS, TOK), F32),
            pltpu.VMEM((TOK, ROWS), BF),
            pltpu.VMEM((2, TOK, ROWS), BF),
            pltpu.VMEM((ROWS, TOK), F32),
            pltpu.VMEM((ROWS, TOK), F32),
            dma((SLOTS,)), dma((SLOTS,)),
            dma((12,)), dma((12,)),
            dma((9,)), dma((9,)),
            dma((SLOTS,)), dma((SLOTS,)),
            dma((SLOTS,)), dma((SLOTS,)),
            dma((SLOTS,)), dma((SLOTS,)),
            dma((3,)), dma((3,)),
            dma((3,)), dma((3,)),
            dma((6 + SLOTS,)),
        ],
        compiler_params=pltpu.CompilerParams(
            collective_id=0, has_side_effects=True, vmem_limit_bytes=64 * 2**20 - 65536
        ),
    )(tokens, cotangent, routes.T, gates.T, w_in, w_out)
    return outs[0], outs[1], outs[2].T, outs[3], outs[4]


def solution(mesh):
    rows = P(("tensor", "context", "dp"), None)
    experts = P(("tensor", "context"), None, None)
    return jax.shard_map(
        shards,
        mesh=mesh,
        in_specs=(rows, rows, rows, experts, experts, rows),
        out_specs=(rows, rows, rows, rows, rows),
        check_vma=False,
    )
```

time: 587 us -> 247 us (0.42)
  waiting for transfers between devices: 357 us -> 0 us
  Pallas kernels: 0 us -> 237 us
  blocking collectives: 81.3 us -> 0 us
  matrix products: 52.9 us -> 0 us
  local copies, waits for them, and re-layouts: 42.9 us -> 7.36 us
  other arithmetic: 32.5 us -> 0 us
  between operations: 14.3 us -> 0.66 us
    pallas_call x0 -> x1, Pallas kernels: none -> 237 us  [shards(): pl.pallas_call(kernel, name='experts', out_shape=(jax.ShapeDtypeStruct((T...]
    reduce_scatter x2 -> x0, waiting for transfers between devices: 217 us -> none  [the longest x1 217 us: shards(): lax.psum_scatter(lax.dot_general(piece, grad_gate_up, (((0,), (0,)), ((),...]
    all_to_all x1 -> x0, waiting for transfers between devices: 140 us -> none  [trade_rows(): lax.all_to_all(buffer, ('tensor', 'context'), split_axis=0, concat_axis=0...]
    all_to_all x1 -> x0, blocking collectives: 81.3 us -> none  [trade_rows(): lax.all_to_all(buffer, ('tensor', 'context'), split_axis=0, concat_axis=0...]
    dot_general x6 -> x0, matrix products: 52.9 us -> none  [the longest x1 17.2 us: shards(): lax.dot_general(grad_gate_up, weight_in, (((1,), (1,)), ((), ())), prefer...]
    gather x5 -> x0, local copies, waits for them, and re-layouts: 21.8 us -> none  [the longest x1 7.66 us: shards(): dx_back.reshape(-1, model_width)[positions]]
    reduce_sum x3 -> x0, other arithmetic: 18.3 us -> none  [the longest x1 10.5 us: shards(): jnp.sum(cotangent[:, None, :].astype(jnp.float32) * out_routes, axis=2)]
    slice x3 -> x0, local copies, waits for them, and re-layouts: 6.24 us -> none  [the longest x1 5.27 us: shards(): dx_back = returned[:, capacity:]]
  transfers between devices with their start and end apart: 3 -> 0, of which waited for: 2 -> 0; matrix products, arithmetic and copies ran while one was open for 14% -> 0% of each run, Pallas kernels for 0% -> 0%
where the time goes in v1:
time: 247 us; the launch traced here: 246 us
  Pallas kernels  237 us (96%)
  local copies, waits for them, and re-layouts  7.36 us (3%)
    pallas_call x1, Pallas kernels, shards(): pl.pallas_call(kernel, name='experts', out_shape=(jax.ShapeDtypeStruct((T...  237 us
    unnamed x11, local copies, waits for them, and re-layouts  7.36 us

profile of v1, /device:TPU:1, one launch (start us, length us, event | category | flops | bytes accessed | tf_op | source)
XLA Modules:
  0.0 245.5 jit_solution(17280531725715525653)
XLA Ops:
  0.6 237.5 %experts.1 = (bf16[128,4096]{1,0:T(8,128)(2,1)}, bf16[128,4096]{1,0:T(8,128)(2,1)}, f32[2,128]{1,0:T(2,128)}, bf16[512,1536]{1,0:T(8,128)(2,1)}, bf16[96,4096]{1...) custom-call(bf16[128,4096]{1,0:T(8,128)(2,1)} %tok_hbm.1, bf16[128,4096]{1,0:T(8,128)(2,1)} %cot_hbm.1, ...), custom_call_target="tpu_custom_call" | custom-call | tf_op jit(solution)/shard_map/experts/pallas_call | solution.py:372
  238.1 0.0 copy-start.2
  238.1 0.0 copy-start
  238.1 2.4 copy.16
  240.6 0.0 copy-start.1
  240.6 2.4 copy.17
  242.9 0.0 copy-done.2
  242.9 0.6 copy.18
  243.5 0.0 copy-done
  243.5 1.1 copy.19
  244.6 0.0 copy-done.1
  244.6 0.9 copy.20
Async XLA Ops:
  238.1 4.8 %copy-start.2 = (f32[2,128]{1,0:T(2,128)S(1)}, f32[2,128]{1,0:T(2,128)}, u32[]{:S(2)}) copy-start(f32[2,128]{1,0:T(2,128)} %get-tuple-element.12) | copy-start | bytes 3076
  238.1 5.3 %copy-start = (bf16[512,1536]{1,0:T(8,128)(2,1)S(1)}, bf16[512,1536]{1,0:T(8,128)(2,1)}, u32[]{:S(2)}) copy-start(bf16[512,1536]{1,0:T(8,128)(2,1)} %get-tuple-element.23) | copy-start | bytes 4718596
  240.6 4.1 %copy-start.1 = (bf16[96,4096]{1,0:T(8,128)(2,1)S(1)}, bf16[96,4096]{1,0:T(8,128)(2,1)}, u32[]{:S(2)}) copy-start(bf16[96,4096]{1,0:T(8,128)(2,1)} %get-tuple-element.24) | copy-start | bytes 2359300

commit v2 on v1

--- a/solution.py
+++ b/solution.py
@@ -16,6 +16,7 @@
 ROWS = SLOTS * CAP
 TOK = 128
 OWN = 12
+ORDER = (2, 1, 3, 0)
 QD = D // 4
 HD = D // 2
 
@@ -129,55 +130,51 @@
     ld_wout.start()
     pl.semaphore_wait(bar, 19)
 
+    def quarter(k):
+        return pl.ds(pl.multiple_of(((z + k) % 4) * QD, QD), QD)
+
     d_cp = {}
-    for j in range(4):
-        g0 = j * 4 * CAP
-
-        @pl.loop(0, 4)
+    for k in ORDER:
+
+        @pl.loop(0, 2)
         def _(n):
-            cs = pl.ds(pl.multiple_of(n * 1024, 1024), 1024)
-            sm = smat[g0:g0 + 4 * CAP, :]
-            a = dot(sm, mixed_ref[:, cs])
-            b = dot(sm, gtok_ref[:, cs]) * gcol[g0:g0 + 4 * CAP, 0:1]
-            send[4 * j:4 * j + 4, :, cs] = join_rows(a, b)
-
-        for m in range(4):
-            i = 4 * j + m
+            cs = pl.ds(pl.multiple_of(((z + k) % 4) * QD + n * 512, 512), 512)
+            a = dot(smat[...], mixed_ref[:, cs])
+            b = dot(smat[...], gtok_ref[:, cs]) * gcol[:, 0:1]
+            send[:, :, cs] = join_rows(a, b)
+
+        for i in range(SLOTS):
+            src, dst = send.at[i, :, quarter(k)], rx.at[i, :, quarter(k)]
+            n = k * SLOTS + i
             if i == OWN:
-                d_cp[i] = pltpu.make_async_copy(send.at[i], rx.at[i], loc.at[4])
+                d_cp[k, i] = pltpu.make_async_copy(src, dst, loc.at[4 + k])
             else:
-                d_cp[i] = remote(send.at[i], rx.at[i], d_ss.at[i], d_rs.at[i], to_expert(i))
-            d_cp[i].start()
-
+                d_cp[k, i] = remote(src, dst, d_ss.at[n], d_rs.at[n], to_expert(i))
+            d_cp[k, i].start()
+
+    fs[...] = jnp.zeros_like(fs)
     z_cp = []
-    for j in (3, 0, 2, 1):
-        for m in range(4):
-            i = 4 * j + m
+    for k in ORDER:
+        for i in range(SLOTS):
             if i == OWN:
-                d_cp[i].wait()
+                d_cp[k, i].wait()
             else:
-                d_cp[i].wait_recv()
-        for k in (1, 2, 3):
-            n = j * 3 + k - 1
-            cols = pl.ds(pl.multiple_of(((z + k) % 4) * QD, QD), QD)
-            cp = remote(
-                rx.at[4 * j:4 * j + 4, :, cols], xdz.at[k - 1, 4 * j:4 * j + 4],
-                z_ss.at[n], z_rs.at[n], z_peer(k),
-            )
+                d_cp[k, i].wait_recv()
+        if k > 0:
+            cp = remote(rx.at[:, :, quarter(k)], xdz.at[k - 1], z_ss.at[k - 1], z_rs.at[k - 1], z_peer(k))
             cp.start()
             z_cp.append(cp)
-
-    ld_win.wait()
-    ld_wout.wait()
-    fs[...] = jnp.zeros_like(fs)
-
-    @pl.loop(0, 8)
-    def _(n):
-        ks = pl.ds(pl.multiple_of(n * 512, 512), 512)
-        xk, dk = split_rows(rx[:, :, ks])
-        fs[0:ROWS, :] += dot(xk, win[ks, 0:F])
-        fs[ROWS:2 * ROWS, :] += dot(xk, win[ks, F:2 * F])
-        fs[2 * ROWS:3 * ROWS, :] += dot_nt(dk, wout[:, ks])
+        if k == ORDER[0]:
+            ld_win.wait()
+            ld_wout.wait()
+
+        @pl.loop(0, 2)
+        def _(n):
+            ks = pl.ds(pl.multiple_of(((z + k) % 4) * QD + n * 512, 512), 512)
+            xk, dk = split_rows(rx[:, :, ks])
+            fs[0:ROWS, :] += dot(xk, win[ks, 0:F])
+            fs[ROWS:2 * ROWS, :] += dot(xk, win[ks, F:2 * F])
+            fs[2 * ROWS:3 * ROWS, :] += dot_nt(dk, wout[:, ks])
 
     @pl.loop(0, 8)
     def _(n):
@@ -200,9 +197,10 @@
             a_cp[p, k] = remote(agb.at[p, 3], agb.at[p, k - 1], a_ss.at[n], a_rs.at[n], z_peer(k))
             a_cp[p, k].start()
 
-    for i in range(SLOTS):
-        if i != OWN:
-            d_cp[i].wait_send()
+    for k in ORDER:
+        for i in range(SLOTS):
+            if i != OWN:
+                d_cp[k, i].wait_send()
 
     @pl.loop(0, 4)
     def _(n):
@@ -216,7 +214,7 @@
     for i in range(SLOTS):
         rows = pl.ds(i * CAP, CAP)
         if i == OWN:
-            s_cp[i] = pltpu.make_async_copy(sval.at[rows], sret.at[rows], loc.at[5])
+            s_cp[i] = pltpu.make_async_copy(sval.at[rows], sret.at[rows], loc.at[8])
         else:
             o_cp[i] = remote(send.at[i, :, 0:HD], ro_hbm.at[i], o_ss.at[i], o_rs.at[i], to_source(i))
             o_cp[i].start()
@@ -323,7 +321,7 @@
     back = []
     for i in range(SLOTS):
         src = send.at[i, :, 0:HD] if i == OWN else ro_hbm.at[i]
-        back.append(pltpu.make_async_copy(src, rx.at[i, :, 0:HD], loc.at[6 + i]))
+        back.append(pltpu.make_async_copy(src, rx.at[i, :, 0:HD], loc.at[9 + i]))
         back[-1].start()
     for cp in back:
         cp.wait()
@@ -341,7 +339,7 @@
     back = []
     for i in range(SLOTS):
         src = send.at[i, :, HD:D] if i == OWN else rdx_hbm.at[i]
-        back.append(pltpu.make_async_copy(src, rx.at[i, :, HD:D], loc.at[6 + i]))
+        back.append(pltpu.make_async_copy(src, rx.at[i, :, HD:D], loc.at[9 + i]))
         back[-1].start()
     for cp in back:
         cp.wait()
@@ -405,15 +403,15 @@
             pltpu.VMEM((2, TOK, ROWS), BF),
             pltpu.VMEM((ROWS, TOK), F32),
             pltpu.VMEM((ROWS, TOK), F32),
-            dma((SLOTS,)), dma((SLOTS,)),
-            dma((12,)), dma((12,)),
+            dma((4 * SLOTS,)), dma((4 * SLOTS,)),
+            dma((3,)), dma((3,)),
             dma((9,)), dma((9,)),
             dma((SLOTS,)), dma((SLOTS,)),
             dma((SLOTS,)), dma((SLOTS,)),
             dma((SLOTS,)), dma((SLOTS,)),
             dma((3,)), dma((3,)),
             dma((3,)), dma((3,)),
-            dma((6 + SLOTS,)),
+            dma((9 + SLOTS,)),
         ],
         compiler_params=pltpu.CompilerParams(
             collective_id=0, has_side_effects=True, vmem_limit_bytes=64 * 2**20 - 65536

time: 247 us -> 219 us (0.89)
  Pallas kernels: 237 us -> 211 us
    pallas_call x1, Pallas kernels: 237 us -> 211 us  [shards(): pl.pallas_call(kernel, name='experts', out_shape=(jax.ShapeDtypeStruct((T...]
where the time goes in v2:
time: 219 us
  Pallas kernels  211 us (96%)
  local copies, waits for them, and re-layouts  7.36 us (3%)
    pallas_call x1, Pallas kernels, shards(): pl.pallas_call(kernel, name='experts', out_shape=(jax.ShapeDtypeStruct((T...  211 us
    unnamed x11, local copies, waits for them, and re-layouts  7.36 us

profile of v2, /device:TPU:1, one launch (start us, length us, event | category | flops | bytes accessed | tf_op | source)
XLA Modules:
  0.0 219.1 jit_solution(13726659956614737701)
XLA Ops:
  0.6 211.1 %experts.1 = (bf16[128,4096]{1,0:T(8,128)(2,1)}, bf16[128,4096]{1,0:T(8,128)(2,1)}, f32[2,128]{1,0:T(2,128)}, bf16[512,1536]{1,0:T(8,128)(2,1)}, bf16[96,4096]{1...) custom-call(bf16[128,4096]{1,0:T(8,128)(2,1)} %tok_hbm.1, bf16[128,4096]{1,0:T(8,128)(2,1)} %cot_hbm.1, ...), custom_call_target="tpu_custom_call" | custom-call | tf_op jit(solution)/shard_map/experts/pallas_call | solution.py:370
  211.7 0.0 copy-start.2
  211.7 0.0 copy-start
  211.8 2.4 %copy.16 = bf16[128,4096]{1,0:T(8,128)(2,1)} copy(bf16[128,4096]{1,0:T(8,128)(2,1)} %get-tuple-element.20) | data formatting | bytes 2097152
  214.2 0.0 copy-start.1
  214.2 2.4 %copy.17 = bf16[128,4096]{1,0:T(8,128)(2,1)} copy(bf16[128,4096]{1,0:T(8,128)(2,1)} %get-tuple-element.21) | data formatting | bytes 2097152
  216.5 0.0 copy-done.2
  216.5 0.6 copy.18
  217.1 0.0 copy-done
  217.1 1.1 copy.19
  218.2 0.0 copy-done.1
  218.2 0.9 copy.20
Async XLA Ops:
  211.7 4.8 %copy-start.2 = (f32[2,128]{1,0:T(2,128)S(1)}, f32[2,128]{1,0:T(2,128)}, u32[]{:S(2)}) copy-start(f32[2,128]{1,0:T(2,128)} %get-tuple-element.12) | copy-start | bytes 3076
  211.7 5.3 %copy-start = (bf16[512,1536]{1,0:T(8,128)(2,1)S(1)}, bf16[512,1536]{1,0:T(8,128)(2,1)}, u32[]{:S(2)}) copy-start(bf16[512,1536]{1,0:T(8,128)(2,1)} %get-tuple-element.23) | copy-start | bytes 4718596
  214.2 4.1 %copy-start.1 = (bf16[96,4096]{1,0:T(8,128)(2,1)S(1)}, bf16[96,4096]{1,0:T(8,128)(2,1)}, u32[]{:S(2)}) copy-start(bf16[96,4096]{1,0:T(8,128)(2,1)} %get-tuple-element.24) | copy-start | bytes 2359300

commit v3 on v2

v3 whole, which is shorter than its diff:
```python
import jax
import jax.numpy as jnp
from jax import lax
from jax.experimental import pallas as pl
from jax.experimental.pallas import tpu as pltpu
from jax.sharding import PartitionSpec as P

MESH = pl.DeviceIdType.MESH
BF = jnp.bfloat16
F32 = jnp.float32

D = 4096
F = 768
CAP = 24
SLOTS = 16
ROWS = SLOTS * CAP
TOK = 128
OWN = 12
PIECES = ((2, 0, 1024), (1, 0, 1024), (3, 0, 1024), (0, 0, 1024))
QD = D // 4
HD = D // 2


def dot(a, b):
    return jnp.dot(a, b, preferred_element_type=F32)


def dot_nt(a, b):
    return lax.dot_general(a, b, (((1,), (1,)), ((), ())), preferred_element_type=F32)


def dot_tn(a, b):
    return lax.dot_general(a, b, (((0,), (0,)), ((), ())), preferred_element_type=F32)


def split_rows(block):
    wide = block.astype(F32)
    n = wide.shape[-1]
    first = wide[:, :CAP, :].reshape(ROWS, n).astype(BF)
    last = wide[:, CAP:, :].reshape(ROWS, n).astype(BF)
    return first, last


def join_rows(first, last):
    n = first.shape[-1]
    s = first.shape[0] // CAP
    return jnp.concatenate([first.reshape(s, CAP, n), last.reshape(s, CAP, n)], axis=1).astype(BF)


def kernel(
    tok_hbm, cot_hbm, routes_ref, gates_ref, win_hbm, wout_hbm,
    mixed_out, gtok_out, ggate_ref, gin_out, gout_out, ro_hbm, rdx_hbm,
    mixed_ref, gtok_ref, gin_ref, gout_ref,
    send, rx, xdz, win, wout, fs, agb, go, gr_in, gr_out, gt_r, pr,
    sel, smat, pack_s, pack_r, gcol, stmat, gmat, sval, sret,
    d_ss, d_rs, z_ss, z_rs, a_ss, a_rs, o_ss, o_rs, x_ss, x_rs, s_ss, s_rs, e_ss, e_rs, t_ss, t_rs,
    g_ss, g_rs, p_ss, p_rs, loc, out_sem,
):
    y = lax.axis_index("tensor")
    c = lax.axis_index("context")
    d = lax.axis_index("dp")
    z = d // 2
    xl = d % 2
    xh = c // 2
    co = c % 2

    def context_of(i):
        return (1 - xh if i % 2 else xh) * 2 + (1 - co if i // 2 % 2 else co)

    def to_expert(i):
        return ((y + 1 + i // 4) % 4, context_of(i), d)

    def to_source(i):
        return ((y + 3 - i // 4) % 4, context_of(i), d)

    def z_peer(k):
        return (y, c, ((z + k) % 4) * 2 + xl)

    pair = (y, c, z * 2 + (1 - xl))
    partner = to_expert(OWN + 1)

    def remote(src, dst, ss, rs, dev):
        return pltpu.make_async_remote_copy(
            src_ref=src, dst_ref=dst, send_sem=ss, recv_sem=rs, device_id=dev, device_id_type=MESH
        )

    ld_tok = pltpu.make_async_copy(tok_hbm, mixed_ref, loc.at[0])
    ld_cot = pltpu.make_async_copy(cot_hbm, gtok_ref, loc.at[1])
    ld_win = pltpu.make_async_copy(win_hbm.at[0], win, loc.at[2])
    ld_wout = pltpu.make_async_copy(wout_hbm.at[0], wout, loc.at[3])
    ld_tok.start()
    ld_cot.start()

    bar = pltpu.get_barrier_semaphore()
    for i in range(SLOTS):
        if i != OWN:
            pl.semaphore_signal(bar, inc=1, device_id=to_expert(i), device_id_type=MESH)
    for k in (1, 2, 3):
        pl.semaphore_signal(bar, inc=1, device_id=z_peer(k), device_id_type=MESH)
    pl.semaphore_signal(bar, inc=1, device_id=pair, device_id_type=MESH)

    pack_s[0:2, :] = routes_ref[...].astype(F32)
    pack_s[2:4, :] = gates_ref[...]
    row = lax.broadcasted_iota(jnp.int32, (ROWS, TOK), 0)
    slot = (row * 683) >> 14
    place = (row - slot * CAP).astype(F32)
    far = slot & 1
    ahead = ((y + 1 + (slot >> 2)) & 3) * 4 + (co ^ ((slot >> 1) & 1))
    before = jnp.where(
        lax.broadcasted_iota(jnp.int32, (TOK, TOK), 0) < lax.broadcasted_iota(jnp.int32, (TOK, TOK), 1),
        1.0, 0.0,
    ).astype(BF)

    def tables(pack, half):
        r0, r1 = pack[0:1, :], pack[1:2, :]
        expert = (ahead + (half ^ far) * 2).astype(F32)
        ids = lax.broadcasted_iota(jnp.int32, (SLOTS, TOK), 0).astype(F32)
        match = jnp.where((ids == r0) | (ids == r1), 1.0, 0.0).astype(BF)
        rank = dot(match, before).astype(BF)
        pick = jnp.where(
            expert[:, :SLOTS] == lax.broadcasted_iota(jnp.int32, (ROWS, SLOTS), 1).astype(F32), 1.0, 0.0
        ).astype(BF)
        here = dot(pick, rank) == place
        s0 = jnp.where((expert == r0) & here, 1.0, 0.0)
        s1 = jnp.where((expert == r1) & here, 1.0, 0.0)
        return s0, s1, s0 * pack[2:3, :] + s1 * pack[3:4, :]

    s0, s1, gsel = tables(pack_s[...], xh)
    sel[0] = s0
    sel[1] = s1
    smat[...] = (s0 + s1).astype(BF)
    gcol[...] = jnp.broadcast_to(jnp.sum(gsel, axis=1, keepdims=True), (ROWS, TOK))

    def put(half, gates, chosen):
        rows = pl.ds(half * TOK, TOK)
        gt = gates.T
        ghi = gt.astype(BF)
        gmat[0, rows, :] = ghi
        gmat[1, rows, :] = (gt - ghi.astype(F32)).astype(BF)
        stmat[rows, :] = chosen.T.astype(BF)

    ld_tok.wait()
    ld_cot.wait()
    ld_win.start()
    ld_wout.start()
    pl.semaphore_wait(bar, 19)

    g_cp = remote(pack_s, pack_r, g_ss.at[0], g_rs.at[0], partner)
    g_cp.start()

    def quarter(k, off, width):
        return pl.ds(pl.multiple_of(((z + k) % 4) * QD + off, 512), width)

    d_cp = {}
    for u, (k, off, width) in enumerate(PIECES):

        @pl.loop(0, width // 512)
        def _(n):
            cs = pl.ds(pl.multiple_of(((z + k) % 4) * QD + off + n * 512, 512), 512)
            a = dot(smat[...], mixed_ref[:, cs])
            b = dot(smat[...], gtok_ref[:, cs]) * gcol[:, 0:1]
            send[:, :, cs] = join_rows(a, b)

        cols = quarter(k, off, width)
        for i in range(SLOTS):
            src, dst = send.at[i, :, cols], rx.at[i, :, cols]
            n = u * SLOTS + i
            if i == OWN:
                d_cp[u, i] = pltpu.make_async_copy(src, dst, loc.at[4 + u])
            else:
                d_cp[u, i] = remote(src, dst, d_ss.at[n], d_rs.at[n], to_expert(i))
            d_cp[u, i].start()

    fs[...] = jnp.zeros_like(fs)
    near = far == 0
    put(
        0, jnp.where(near, sel[0] * pack_s[2:3, :] + sel[1] * pack_s[3:4, :], 0.0),
        jnp.where(near, sel[0] + sel[1], 0.0),
    )
    g_cp.wait()
    t0, t1, tsel = tables(pack_r[...], 1 - xh)
    put(1, jnp.where(near, 0.0, tsel), jnp.where(near, 0.0, t0 + t1))
    z_cp = []
    for u, (k, off, width) in enumerate(PIECES):
        for i in range(SLOTS):
            if i == OWN:
                d_cp[u, i].wait()
            else:
                d_cp[u, i].wait_recv()
        if k > 0:
            cp = remote(
                rx.at[:, :, quarter(k, off, width)], xdz.at[k - 1, :, :, pl.ds(off, width)],
                z_ss.at[u], z_rs.at[u], z_peer(k),
            )
            cp.start()
            z_cp.append(cp)
        if u == 0:
            ld_win.wait()
            ld_wout.wait()

        @pl.loop(0, width // 512)
        def _(n):
            ks = pl.ds(pl.multiple_of(((z + k) % 4) * QD + off + n * 512, 512), 512)
            xk, dk = split_rows(rx[:, :, ks])
            fs[0:ROWS, :] += dot(xk, win[ks, 0:F])
            fs[ROWS:2 * ROWS, :] += dot(xk, win[ks, F:2 * F])
            fs[2 * ROWS:3 * ROWS, :] += dot_nt(dk, wout[:, ks])

    @pl.loop(0, 8)
    def _(n):
        r = pl.multiple_of(n * 48, 48)
        g = fs[pl.ds(r, 48), :]
        u = fs[pl.ds(r + ROWS, 48), :]
        dh = fs[pl.ds(r + 2 * ROWS, 48), :]
        s = jax.nn.sigmoid(g)
        h = (g * s * u).astype(BF)
        rs = pl.ds(r, 48)
        agb[2, 3, rs, :] = h
        agb[0, 3, rs, :] = (dh * u * s * (1.0 + g * (1.0 - s))).astype(BF)
        agb[1, 3, rs, :] = (dh * g * s).astype(BF)
        sval[rs, :] = jnp.broadcast_to(jnp.sum(h.astype(F32) * dh, axis=1, keepdims=True), (48, TOK))

    a_cp = {}

    def gather_start(p):
        for k in (1, 3):
            n = p * 4 + k
            a_cp[p, k] = remote(agb.at[p, 3], agb.at[p, k - 1], a_ss.at[n], a_rs.at[n], z_peer(k))
            a_cp[p, k].start()

    def gather_pass(p):
        for k, cols in ((1, pl.ds(0, F // 2)), (3, pl.ds(F // 2, F // 2))):
            a_cp[p, k].wait_recv()
            n = p * 4 + k - 1
            a_cp[p, k - 1] = remote(
                agb.at[p, k - 1, :, cols], agb.at[p, 1, :, cols], a_ss.at[n], a_rs.at[n], z_peer(k)
            )
            a_cp[p, k - 1].start()

    def gather_end(p):
        a_cp[p, 0].wait_recv()
        a_cp[p, 2].wait_recv()

    gather_start(2)
    gather_start(0)

    for u in range(len(PIECES)):
        for i in range(SLOTS):
            if i != OWN:
                d_cp[u, i].wait_send()

    o_cp, s_cp = {}, {}

    def give(t, q, buf, ss, rs):
        cols = pl.ds(q * QD, QD)
        for p in range(8):
            src, dst = send.at[8 * t + p, :, cols], buf.at[pl.ds(p * 48, 48), cols]
            n = q * 8 + p
            if 2 * p == OWN:
                cp = pltpu.make_async_copy(src, dst, loc.at[11 + 4 * t + q])
            else:
                cp = remote(src, dst, ss.at[n], rs.at[n], to_source(2 * p))
            cp.start()
            o_cp[t, q, p] = cp

    for q in range(4):

        @pl.loop(0, 2)
        def _(n):
            cs = pl.ds(pl.multiple_of(q * QD + n * 512, 512), 512)
            send[0:8, :, cs] = dot(agb[2, 3], wout[:, cs]).astype(BF).reshape(8, 48, 512)

        give(0, q, ro_hbm, o_ss, o_rs)

    for i in range(SLOTS):
        rows = pl.ds(i * CAP, CAP)
        if i == OWN:
            s_cp[i] = pltpu.make_async_copy(sval.at[rows], sret.at[rows], loc.at[10])
        else:
            s_cp[i] = remote(sval.at[rows], sret.at[rows], s_ss.at[i], s_rs.at[i], to_source(i))
        s_cp[i].start()

    for q in range(4):

        @pl.loop(0, 2)
        def _(n):
            cs = pl.ds(pl.multiple_of(q * QD + n * 512, 512), 512)
            dx = dot_nt(agb[0, 3], win[cs, 0:F]) + dot_nt(agb[1, 3], win[cs, F:2 * F])
            send[8:16, :, cs] = dx.astype(BF).reshape(8, 48, 512)

        give(1, q, rdx_hbm, x_ss, x_rs)

    p_cp = {}

    def relay(t, q):
        cols = pl.ds(q * QD, QD)
        buf = rdx_hbm if t else ro_hbm
        for p in range(8):
            if 2 * p == OWN:
                o_cp[t, q, p].wait()
            else:
                o_cp[t, q, p].wait_recv()
        ld = pltpu.make_async_copy(buf.at[:, cols], wout.at[256:640, cols], loc.at[19 + 4 * t + q])
        ld.start()
        ld.wait()
        own = gtok_ref if t else mixed_ref

        @pl.loop(0, 2)
        def _(n):
            cs = pl.ds(pl.multiple_of(q * QD + n * 512, 512), 512)
            rows = wout[256:640, cs]
            if t:
                part = dot(stmat[...], rows)
            else:
                part = dot(gmat[0], rows) + dot(gmat[1], rows)
            own[:, cs] = part[0:TOK].astype(BF)
            wout[TOK * t:TOK * (t + 1), cs] = part[TOK:2 * TOK].astype(BF)

        n = 4 * t + q
        p_cp[t, q] = remote(
            wout.at[TOK * t:TOK * (t + 1), cols], pr.at[t, :, cols], p_ss.at[n], p_rs.at[n], partner
        )
        p_cp[t, q].start()

    own0 = z * QD
    e_cp = {}
    GS = 512
    GT = 896

    DC = 1280
    XT = 2816

    def arrange():
        for cp in z_cp:
            cp.wait()
        for s in range(4):

            @pl.loop(0, 4)
            def _(n):
                n0 = pl.multiple_of(n * 256, 256)
                if s < 3:
                    blk = xdz[s, :, :, pl.ds(n0, 256)]
                else:
                    blk = rx[:, :, pl.ds(pl.multiple_of(own0 + n0, 256), 256)]
                xk, dk = split_rows(blk)
                win[DC + s * ROWS:DC + (s + 1) * ROWS, pl.ds(n0, 256)] = dk
                win[pl.ds(XT + n0, 256), s * ROWS:(s + 1) * ROWS] = xk.T

    def grad_out():
        gather_end(2)

        @pl.loop(0, 3)
        def _(n):
            n0 = pl.multiple_of(n * 256, 256)
            h = agb[2, :, :, pl.ds(n0, 256)].reshape(4 * ROWS, 256)
            go[pl.ds(n0, 256), :] = dot_tn(h, win[DC:DC + 4 * ROWS, 0:QD])

        for q in range(4):
            r = pl.multiple_of(q * 192 + (1 - xl) * 96, 96)
            win[GS + q * 96:GS + (q + 1) * 96, 0:QD] = go[pl.ds(r, 96), :].astype(BF)
        e_cp[2] = remote(win.at[GS:GS + 384, 0:QD], gr_out, e_ss.at[2], e_rs.at[2], pair)
        e_cp[2].start()

    def grad_in(p):
        gather_end(p)

        def half(side, store):
            @pl.loop(0, 2)
            def _(n):
                n0 = pl.multiple_of(n * 256, 256)
                r = pl.multiple_of(XT + side * 512 + n0, 256)
                store(n0, dot(win[pl.ds(r, 256), :], agb[p].reshape(4 * ROWS, F)))

        def store_send(n0, acc):
            win[pl.ds(n0, 256), p * F:(p + 1) * F] = acc.astype(BF)

        def store_own(n0, acc):
            fs[pl.ds(p * 512 + n0, 256), :] = acc

        half(1 - xl, store_send)
        e_cp[p] = remote(win.at[0:512, p * F:(p + 1) * F], gr_in.at[p], e_ss.at[p], e_rs.at[p], pair)
        e_cp[p].start()
        half(xl, store_own)

    t_cp = []

    def out_rows():
        e_cp[2].wait()
        for q in range(4):
            r = pl.multiple_of(q * 192 + xl * 96, 96)
            win[GT + q * 96:GT + (q + 1) * 96, 0:QD] = (
                go[pl.ds(r, 96), :] + gr_out[q * 96:(q + 1) * 96, :].astype(F32)
            ).astype(BF)
        for k in (1, 2, 3):
            r = pl.multiple_of(GT + ((z + k) % 4) * 96, 32)
            cp = remote(
                win.at[pl.ds(r, 96), 0:QD], gt_r.at[k - 1], t_ss.at[k - 1], t_rs.at[k - 1], z_peer(k)
            )
            cp.start()
            t_cp.append(cp)
        gout_ref[:, pl.ds(pl.multiple_of(own0, QD), QD)] = win[pl.ds(pl.multiple_of(GT + z * 96, 32), 96), 0:QD]

    relay(0, 0)
    relay(0, 1)
    gather_pass(2)
    gather_start(1)
    relay(0, 2)
    relay(0, 3)
    gather_pass(0)
    relay(1, 0)
    arrange()
    grad_out()
    relay(1, 1)
    gather_pass(1)
    relay(1, 2)
    grad_in(0)
    relay(1, 3)
    grad_in(1)
    out_rows()

    for i in range(SLOTS):
        s_cp[i].wait()
    for k in range(2):
        ggate_ref[k:k + 1, :] = (
            jnp.sum(sel[k] * sret[...], axis=0, keepdims=True) / gates_ref[k:k + 1, :]
        )
    out_cp = []

    def leave(src, dst):
        cp = pltpu.make_async_copy(src, dst, out_sem.at[len(out_cp)])
        cp.start()
        out_cp.append(cp)

    for k in (1, 2, 3):
        t_cp[k - 1].wait()
        col = pl.multiple_of(((z + 4 - k) % 4) * QD, QD)
        gout_ref[:, pl.ds(col, QD)] = gt_r[k - 1]
    leave(gout_ref, gout_out)
    for t in range(2):
        own = gtok_ref if t else mixed_ref
        for q in range(4):
            p_cp[t, q].wait()
            cs = pl.ds(q * QD, QD)
            own[:, cs] = (own[:, cs].astype(F32) + pr[t, :, cs].astype(F32)).astype(BF)
        leave(own, gtok_out if t else mixed_out)
    for p in range(2):
        e_cp[p].wait()
        cs = pl.ds(p * F, F)
        gin_ref[:, cs] = (fs[p * 512:(p + 1) * 512, :] + gr_in[p].astype(F32)).astype(BF)
        leave(gin_ref.at[:, cs], gin_out.at[:, cs])

    for p in range(3):
        for k in range(4):
            a_cp[p, k].wait_send()
    for t in range(2):
        for q in range(4):
            for p in range(8):
                if 2 * p != OWN:
                    o_cp[t, q, p].wait_send()
    for cp in out_cp:
        cp.wait()


def hand_over(*refs):
    ins, outs, held, sems = refs[:5], refs[5:10], refs[10:15], refs[15]
    loads = [pltpu.make_async_copy(ins[n], held[n], sems.at[n]) for n in range(5)]
    stores = [pltpu.make_async_copy(held[n], outs[n], sems.at[5 + n]) for n in range(5)]
    for cp in loads:
        cp.start()
    for n in range(5):
        loads[n].wait()
        stores[n].start()
    for cp in stores:
        cp.wait()


def shards(tokens, gates, routes, w_in, w_out, cotangent):
    hbm = pl.BlockSpec(memory_space=pl.ANY)
    vm = pl.BlockSpec(memory_space=pltpu.VMEM)
    dma = pltpu.SemaphoreType.DMA
    outs = pl.pallas_call(
        kernel,
        name="experts",
        out_shape=(
            jax.ShapeDtypeStruct((TOK, D), BF),
            jax.ShapeDtypeStruct((TOK, D), BF),
            jax.ShapeDtypeStruct((2, TOK), F32),
            jax.ShapeDtypeStruct((512, 2 * F), BF),
            jax.ShapeDtypeStruct((96, D), BF),
            jax.ShapeDtypeStruct((ROWS, D), BF),
            jax.ShapeDtypeStruct((ROWS, D), BF),
        ),
        in_specs=[hbm, hbm, vm, vm, hbm, hbm],
        out_specs=(hbm, hbm, vm, hbm, hbm, hbm, hbm),
        scratch_shapes=[
            pltpu.VMEM((TOK, D), BF),
            pltpu.VMEM((TOK, D), BF),
            pltpu.VMEM((512, 2 * F), BF),
            pltpu.VMEM((96, D), BF),
            pltpu.VMEM((SLOTS, 48, D), BF),
            pltpu.VMEM((SLOTS, 48, D), BF),
            pltpu.VMEM((3, SLOTS, 48, QD), BF),
            pltpu.VMEM((D, 2 * F), BF),
            pltpu.VMEM((F, D), BF),
            pltpu.VMEM((3 * ROWS, F), F32),
            pltpu.VMEM((3, 4, ROWS, F), BF),
            pltpu.VMEM((F, QD), F32),
            pltpu.VMEM((2, 512, F), BF),
            pltpu.VMEM((384, QD), BF),
            pltpu.VMEM((3, 96, QD), BF),
            pltpu.VMEM((2, TOK, D), BF),
            pltpu.VMEM((2, ROWS, TOK), F32),
            pltpu.VMEM((ROWS, TOK), BF),
            pltpu.VMEM((8, TOK), F32),
            pltpu.VMEM((8, TOK), F32),
            pltpu.VMEM((ROWS, TOK), F32),
            pltpu.VMEM((2 * TOK, ROWS), BF),
            pltpu.VMEM((2, 2 * TOK, ROWS), BF),
            pltpu.VMEM((ROWS, TOK), F32),
            pltpu.VMEM((ROWS, TOK), F32),
            dma((len(PIECES) * SLOTS,)), dma((len(PIECES) * SLOTS,)),
            dma((len(PIECES),)), dma((len(PIECES),)),
            dma((12,)), dma((12,)),
            dma((32,)), dma((32,)),
            dma((32,)), dma((32,)),
            dma((SLOTS,)), dma((SLOTS,)),
            dma((3,)), dma((3,)),
            dma((3,)), dma((3,)),
            dma((1,)), dma((1,)),
            dma((8,)), dma((8,)),
            dma((27,)),
            dma((5,)),
        ],
        compiler_params=pltpu.CompilerParams(
            collective_id=0, has_side_effects=True, vmem_limit_bytes=64 * 2**20 - 65536
        ),
    )(tokens, cotangent, routes.T, gates.T, w_in, w_out)
    outs = pl.pallas_call(
        hand_over,
        name="hand_over",
        out_shape=tuple(jax.ShapeDtypeStruct(o.shape, o.dtype) for o in outs[:5]),
        in_specs=[hbm] * 5,
        out_specs=(hbm,) * 5,
        scratch_shapes=[pltpu.VMEM(o.shape, o.dtype) for o in outs[:5]] + [dma((10,))],
    )(*outs[:5])
    return outs[0], outs[1], outs[2].T, outs[3], outs[4]


def solution(mesh):
    rows = P(("tensor", "context", "dp"), None)
    experts = P(("tensor", "context"), None, None)
    return jax.shard_map(
        shards,
        mesh=mesh,
        in_specs=(rows, rows, rows, experts, experts, rows),
        out_specs=(rows, rows, rows, rows, rows),
        check_vma=False,
    )
```

time: 219 us -> 215 us (0.982)
  local copies, waits for them, and re-layouts: 7.36 us -> 0 us
  Pallas kernels: 211 us -> 214 us
    unnamed x11 -> x0, local copies, waits for them, and re-layouts: 7.36 us -> none
    pallas_call x0 -> x1, Pallas kernels: none -> 3.54 us  [shards(): pl.pallas_call(hand_over, name='hand_over', out_shape=tuple((jax.ShapeDty...]
where the time goes in v3:
time: 215 us
  Pallas kernels  214 us (100%)
    pallas_call x1, Pallas kernels, shards(): pl.pallas_call(kernel, name='experts', out_shape=(jax.ShapeDtypeStruct((T...  210 us

profile of v3, /device:TPU:1, one launch (start us, length us, event | category | flops | bytes accessed | tf_op | source)
XLA Modules:
  0.0 214.7 jit_solution(8619940818109465017)
XLA Ops:
  0.6 210.4 %experts.1 = (bf16[128,4096]{1,0:T(8,128)(2,1)}, bf16[128,4096]{1,0:T(8,128)(2,1)}, f32[2,128]{1,0:T(2,128)}, bf16[512,1536]{1,0:T(8,128)(2,1)}, bf16[96,4096]{1...) custom-call(bf16[128,4096]{1,0:T(8,128)(2,1)} %tok_hbm.1, bf16[128,4096]{1,0:T(8,128)(2,1)} %cot_hbm.1, ...), custom_call_target="tpu_custom_call" | custom-call | tf_op jit(solution)/shard_map/experts/pallas_call | solution.py:481
  211.0 3.5 %hand_over.1 = (bf16[128,4096]{1,0:T(8,128)(2,1)}, bf16[128,4096]{1,0:T(8,128)(2,1)}, f32[2,128]{1,0:T(2,128)}, bf16[512,1536]{1,0:T(8,128)(2,1)}, bf16[96,4096]{1,0:T(8,128)(2,1)}) custom-call(bf16[128,4096]{1,0:T(8,128)(2,1)} %get-tuple-element.15.refs_0_, bf16[128,4096]{1,0:T(8,128)(2,1)} %get-tuple-element.16.refs_1_, ...), custom_call_target="tpu_custom_call" | custom-call | tf_op jit(solution)/shard_map/hand_over/pallas_call | solution.py:538

commit v4 on v3

--- a/solution.py
+++ b/solution.py
@@ -15,7 +15,7 @@
 SLOTS = 16
 ROWS = SLOTS * CAP
 TOK = 128
-OWN = 12
+OWN = 6
 PIECES = ((2, 0, 1024), (1, 0, 1024), (3, 0, 1024), (0, 0, 1024))
 QD = D // 4
 HD = D // 2
@@ -35,9 +35,9 @@
 
 def split_rows(block):
     wide = block.astype(F32)
-    n = wide.shape[-1]
-    first = wide[:, :CAP, :].reshape(ROWS, n).astype(BF)
-    last = wide[:, CAP:, :].reshape(ROWS, n).astype(BF)
+    rows, n = wide.shape[0] * CAP, wide.shape[-1]
+    first = wide[:, :CAP, :].reshape(rows, n).astype(BF)
+    last = wide[:, CAP:, :].reshape(rows, n).astype(BF)
     return first, last
 
 
@@ -49,11 +49,11 @@
 
 def kernel(
     tok_hbm, cot_hbm, routes_ref, gates_ref, win_hbm, wout_hbm,
-    mixed_out, gtok_out, ggate_ref, gin_out, gout_out, ro_hbm, rdx_hbm,
+    mixed_out, gtok_out, ggate_ref, gin_out, gout_out, ro_hbm,
     mixed_ref, gtok_ref, gin_ref, gout_ref,
     send, rx, xdz, win, wout, fs, agb, go, gr_in, gr_out, gt_r, pr,
     sel, smat, pack_s, pack_r, gcol, stmat, gmat, sval, sret,
-    d_ss, d_rs, z_ss, z_rs, a_ss, a_rs, o_ss, o_rs, x_ss, x_rs, s_ss, s_rs, e_ss, e_rs, t_ss, t_rs,
+    d_ss, d_rs, z_ss, z_rs, a_ss, a_rs, o_ss, o_rs, s_ss, s_rs, e_ss, e_rs, t_ss, t_rs,
     g_ss, g_rs, p_ss, p_rs, loc, out_sem,
 ):
     y = lax.axis_index("tensor")
@@ -65,19 +65,19 @@
     co = c % 2
 
     def context_of(i):
-        return (1 - xh if i % 2 else xh) * 2 + (1 - co if i // 2 % 2 else co)
+        return (1 - xh if i // 8 else xh) * 2 + (1 - co if i % 2 else co)
 
     def to_expert(i):
-        return ((y + 1 + i // 4) % 4, context_of(i), d)
+        return ((y + 1 + i % 8 // 2) % 4, context_of(i), d)
 
     def to_source(i):
-        return ((y + 3 - i // 4) % 4, context_of(i), d)
+        return ((y + 3 - i % 8 // 2) % 4, context_of(i), d)
 
     def z_peer(k):
         return (y, c, ((z + k) % 4) * 2 + xl)
 
     pair = (y, c, z * 2 + (1 - xl))
-    partner = to_expert(OWN + 1)
+    partner = to_expert(OWN + 8)
 
     def remote(src, dst, ss, rs, dev):
         return pltpu.make_async_remote_copy(
@@ -104,8 +104,8 @@
     row = lax.broadcasted_iota(jnp.int32, (ROWS, TOK), 0)
     slot = (row * 683) >> 14
     place = (row - slot * CAP).astype(F32)
-    far = slot & 1
-    ahead = ((y + 1 + (slot >> 2)) & 3) * 4 + (co ^ ((slot >> 1) & 1))
+    far = slot >> 3
+    ahead = ((y + 1 + ((slot >> 1) & 3)) & 3) * 4 + (co ^ (slot & 1))
     before = jnp.where(
         lax.broadcasted_iota(jnp.int32, (TOK, TOK), 0) < lax.broadcasted_iota(jnp.int32, (TOK, TOK), 1),
         1.0, 0.0,
@@ -131,13 +131,16 @@
     smat[...] = (s0 + s1).astype(BF)
     gcol[...] = jnp.broadcast_to(jnp.sum(gsel, axis=1, keepdims=True), (ROWS, TOK))
 
+    HALF = ROWS // 2
+
     def put(half, gates, chosen):
         rows = pl.ds(half * TOK, TOK)
+        cut = slice(half * HALF, (half + 1) * HALF)
         gt = gates.T
         ghi = gt.astype(BF)
-        gmat[0, rows, :] = ghi
-        gmat[1, rows, :] = (gt - ghi.astype(F32)).astype(BF)
-        stmat[rows, :] = chosen.T.astype(BF)
+        gmat[0, rows, :] = ghi[:, cut]
+        gmat[1, rows, :] = (gt - ghi.astype(F32)).astype(BF)[:, cut]
+        stmat[rows, :] = chosen.T.astype(BF)[:, cut]
 
     ld_tok.wait()
     ld_cot.wait()
@@ -172,14 +175,10 @@
             d_cp[u, i].start()
 
     fs[...] = jnp.zeros_like(fs)
-    near = far == 0
-    put(
-        0, jnp.where(near, sel[0] * pack_s[2:3, :] + sel[1] * pack_s[3:4, :], 0.0),
-        jnp.where(near, sel[0] + sel[1], 0.0),
-    )
+    put(0, sel[0] * pack_s[2:3, :] + sel[1] * pack_s[3:4, :], sel[0] + sel[1])
     g_cp.wait()
     t0, t1, tsel = tables(pack_r[...], 1 - xh)
-    put(1, jnp.where(near, 0.0, tsel), jnp.where(near, 0.0, t0 + t1))
+    put(1, tsel, t0 + t1)
     z_cp = []
     for u, (k, off, width) in enumerate(PIECES):
         for i in range(SLOTS):
@@ -251,27 +250,37 @@
 
     o_cp, s_cp = {}, {}
 
-    def give(t, q, buf, ss, rs):
-        cols = pl.ds(q * QD, QD)
-        for p in range(8):
-            src, dst = send.at[8 * t + p, :, cols], buf.at[pl.ds(p * 48, 48), cols]
-            n = q * 8 + p
-            if 2 * p == OWN:
-                cp = pltpu.make_async_copy(src, dst, loc.at[11 + 4 * t + q])
-            else:
-                cp = remote(src, dst, ss.at[n], rs.at[n], to_source(2 * p))
-            cp.start()
-            o_cp[t, q, p] = cp
-
-    for q in range(4):
-
-        @pl.loop(0, 2)
-        def _(n):
-            cs = pl.ds(pl.multiple_of(q * QD + n * 512, 512), 512)
-            send[0:8, :, cs] = dot(agb[2, 3], wout[:, cs]).astype(BF).reshape(8, 48, 512)
-
-        give(0, q, ro_hbm, o_ss, o_rs)
-
+    def give(t, f):
+        top = f * HALF
+        for q in range(2):
+
+            @pl.loop(0, 2)
+            def _(n):
+                parts = []
+                for side in range(2):
+                    cs = pl.ds(pl.multiple_of((2 * q + side) * QD + n * 512, 512), 512)
+                    if t:
+                        part = dot_nt(agb[0, 3, top:top + HALF, :], win[cs, 0:F])
+                        part += dot_nt(agb[1, 3, top:top + HALF, :], win[cs, F:2 * F])
+                    else:
+                        part = dot(agb[2, 3, top:top + HALF, :], wout[:, cs])
+                    parts.append(part)
+                ws = pl.ds(pl.multiple_of(t * HD + q * QD + n * 512, 512), 512)
+                send[8 * f:8 * f + 8, :, ws] = join_rows(*parts)
+
+            for p in range(8):
+                src = send.at[8 * f + p, :, pl.ds(t * HD + q * QD, QD)]
+                dst = ro_hbm.at[pl.ds((2 * t + f) * ROWS + p * 48, 48), pl.ds(q * QD, QD)]
+                n = ((t * 2 + f) * 2 + q) * 8 + p
+                if p == OWN:
+                    cp = pltpu.make_async_copy(src, dst, loc.at[11 + (t * 2 + f) * 2 + q])
+                else:
+                    cp = remote(src, dst, o_ss.at[n], o_rs.at[n], to_source(p))
+                cp.start()
+                o_cp[t, f, q, p] = cp
+
+    give(0, 1)
+    give(1, 1)
     for i in range(SLOTS):
         rows = pl.ds(i * CAP, CAP)
         if i == OWN:
@@ -279,48 +288,50 @@
         else:
             s_cp[i] = remote(sval.at[rows], sret.at[rows], s_ss.at[i], s_rs.at[i], to_source(i))
         s_cp[i].start()
-
-    for q in range(4):
+    give(0, 0)
+    give(1, 0)
+
+    p_cp = {}
+
+    def relay(t, f, q):
+        for p in range(8):
+            if p == OWN:
+                o_cp[t, f, q, p].wait()
+            else:
+                o_cp[t, f, q, p].wait_recv()
+        cols = pl.ds(q * QD, QD)
+        ld = pltpu.make_async_copy(
+            ro_hbm.at[pl.ds((2 * t + f) * ROWS, ROWS), cols], wout.at[256:640, cols],
+            loc.at[19 + (t * 2 + f) * 2 + q],
+        )
+        ld.start()
+        ld.wait()
+        if f == 0:
+            p_cp[t, q].wait()
+        own = gtok_ref if t else mixed_ref
+        rows = pl.ds(f * TOK, TOK)
 
         @pl.loop(0, 2)
         def _(n):
-            cs = pl.ds(pl.multiple_of(q * QD + n * 512, 512), 512)
-            dx = dot_nt(agb[0, 3], win[cs, 0:F]) + dot_nt(agb[1, 3], win[cs, F:2 * F])
-            send[8:16, :, cs] = dx.astype(BF).reshape(8, 48, 512)
-
-        give(1, q, rdx_hbm, x_ss, x_rs)
-
-    p_cp = {}
-
-    def relay(t, q):
-        cols = pl.ds(q * QD, QD)
-        buf = rdx_hbm if t else ro_hbm
-        for p in range(8):
-            if 2 * p == OWN:
-                o_cp[t, q, p].wait()
-            else:
-                o_cp[t, q, p].wait_recv()
-        ld = pltpu.make_async_copy(buf.at[:, cols], wout.at[256:640, cols], loc.at[19 + 4 * t + q])
-        ld.start()
-        ld.wait()
-        own = gtok_ref if t else mixed_ref
-
-        @pl.loop(0, 2)
-        def _(n):
-            cs = pl.ds(pl.multiple_of(q * QD + n * 512, 512), 512)
-            rows = wout[256:640, cs]
-            if t:
-                part = dot(stmat[...], rows)
-            else:
-                part = dot(gmat[0], rows) + dot(gmat[1], rows)
-            own[:, cs] = part[0:TOK].astype(BF)
-            wout[TOK * t:TOK * (t + 1), cs] = part[TOK:2 * TOK].astype(BF)
-
-        n = 4 * t + q
-        p_cp[t, q] = remote(
-            wout.at[TOK * t:TOK * (t + 1), cols], pr.at[t, :, cols], p_ss.at[n], p_rs.at[n], partner
-        )
-        p_cp[t, q].start()
+            ws = pl.ds(pl.multiple_of(q * QD + n * 512, 512), 512)
+            for side, block in enumerate(split_rows(wout[256:640, ws].reshape(8, 48, 512))):
+                cs = pl.ds(pl.multiple_of((2 * q + side) * QD + n * 512, 512), 512)
+                if t:
+                    part = dot(stmat[rows, :], block)
+                else:
+                    part = dot(gmat[0, rows, :], block) + dot(gmat[1, rows, :], block)
+                if f:
+                    wout[TOK * t:TOK * (t + 1), cs] = part.astype(BF)
+                else:
+                    own[:, cs] = (part + pr[t, :, cs].astype(F32)).astype(BF)
+
+        if f:
+            n = 2 * t + q
+            cs = pl.ds(q * HD, HD)
+            p_cp[t, q] = remote(
+                wout.at[TOK * t:TOK * (t + 1), cs], pr.at[t, :, cs], p_ss.at[n], p_rs.at[n], partner
+            )
+            p_cp[t, q].start()
 
     own0 = z * QD
     e_cp = {}
@@ -400,23 +411,23 @@
             t_cp.append(cp)
         gout_ref[:, pl.ds(pl.multiple_of(own0, QD), QD)] = win[pl.ds(pl.multiple_of(GT + z * 96, 32), 96), 0:QD]
 
-    relay(0, 0)
-    relay(0, 1)
+    relay(0, 1, 0)
+    relay(0, 1, 1)
     gather_pass(2)
     gather_start(1)
-    relay(0, 2)
-    relay(0, 3)
+    relay(1, 1, 0)
+    relay(1, 1, 1)
+    arrange()
     gather_pass(0)
-    relay(1, 0)
-    arrange()
     grad_out()
-    relay(1, 1)
+    relay(0, 0, 0)
     gather_pass(1)
-    relay(1, 2)
     grad_in(0)
-    relay(1, 3)
     grad_in(1)
+    relay(0, 0, 1)
     out_rows()
+    relay(1, 0, 0)
+    relay(1, 0, 1)
 
     for i in range(SLOTS):
         s_cp[i].wait()
@@ -436,13 +447,8 @@
         col = pl.multiple_of(((z + 4 - k) % 4) * QD, QD)
         gout_ref[:, pl.ds(col, QD)] = gt_r[k - 1]
     leave(gout_ref, gout_out)
-    for t in range(2):
-        own = gtok_ref if t else mixed_ref
-        for q in range(4):
-            p_cp[t, q].wait()
-            cs = pl.ds(q * QD, QD)
-            own[:, cs] = (own[:, cs].astype(F32) + pr[t, :, cs].astype(F32)).astype(BF)
-        leave(own, gtok_out if t else mixed_out)
+    leave(mixed_ref, mixed_out)
+    leave(gtok_ref, gtok_out)
     for p in range(2):
         e_cp[p].wait()
         cs = pl.ds(p * F, F)
@@ -452,11 +458,9 @@
     for p in range(3):
         for k in range(4):
             a_cp[p, k].wait_send()
-    for t in range(2):
-        for q in range(4):
-            for p in range(8):
-                if 2 * p != OWN:
-                    o_cp[t, q, p].wait_send()
+    for n, cp in o_cp.items():
+        if n[3] != OWN:
+            cp.wait_send()
     for cp in out_cp:
         cp.wait()
 
@@ -487,11 +491,10 @@
             jax.ShapeDtypeStruct((2, TOK), F32),
             jax.ShapeDtypeStruct((512, 2 * F), BF),
             jax.ShapeDtypeStruct((96, D), BF),
-            jax.ShapeDtypeStruct((ROWS, D), BF),
-            jax.ShapeDtypeStruct((ROWS, D), BF),
+            jax.ShapeDtypeStruct((4 * ROWS, HD), BF),
         ),
         in_specs=[hbm, hbm, vm, vm, hbm, hbm],
-        out_specs=(hbm, hbm, vm, hbm, hbm, hbm, hbm),
+        out_specs=(hbm, hbm, vm, hbm, hbm, hbm),
         scratch_shapes=[
             pltpu.VMEM((TOK, D), BF),
             pltpu.VMEM((TOK, D), BF),
@@ -514,20 +517,19 @@
             pltpu.VMEM((8, TOK), F32),
             pltpu.VMEM((8, TOK), F32),
             pltpu.VMEM((ROWS, TOK), F32),
-            pltpu.VMEM((2 * TOK, ROWS), BF),
-            pltpu.VMEM((2, 2 * TOK, ROWS), BF),
+            pltpu.VMEM((2 * TOK, ROWS // 2), BF),
+            pltpu.VMEM((2, 2 * TOK, ROWS // 2), BF),
             pltpu.VMEM((ROWS, TOK), F32),
             pltpu.VMEM((ROWS, TOK), F32),
             dma((len(PIECES) * SLOTS,)), dma((len(PIECES) * SLOTS,)),
             dma((len(PIECES),)), dma((len(PIECES),)),
             dma((12,)), dma((12,)),
-            dma((32,)), dma((32,)),
-            dma((32,)), dma((32,)),
+            dma((64,)), dma((64,)),
             dma((SLOTS,)), dma((SLOTS,)),
             dma((3,)), dma((3,)),
             dma((3,)), dma((3,)),
             dma((1,)), dma((1,)),
-            dma((8,)), dma((8,)),
+            dma((4,)), dma((4,)),
             dma((27,)),
             dma((5,)),
         ],

time: 215 us -> 205 us (0.953)
  Pallas kernels: 214 us -> 204 us
    pallas_call x1, Pallas kernels: 210 us -> 200 us  [shards(): pl.pallas_call(kernel, name='experts', out_shape=(jax.ShapeDtypeStruct((T...]
where the time goes in v4:
time: 205 us
  Pallas kernels  204 us (100%)
    pallas_call x1, Pallas kernels, shards(): pl.pallas_call(kernel, name='experts', out_shape=(jax.ShapeDtypeStruct((T...  200 us

profile of v4, /device:TPU:1, one launch (start us, length us, event | category | flops | bytes accessed | tf_op | source)
XLA Modules:
  0.0 204.6 jit_solution(12839349964160268425)
XLA Ops:
  0.6 200.3 %experts.1 = (bf16[128,4096]{1,0:T(8,128)(2,1)}, bf16[128,4096]{1,0:T(8,128)(2,1)}, f32[2,128]{1,0:T(2,128)}, bf16[512,1536]{1,0:T(8,128)(2,1)}, bf16[96,4096]{1,0:T(8,128)(2,1)}, /*index=5*/bf16[1536,2048]{1,0:T(8,128)(2,1)}) custom-call(bf16[128,4096]{1,0:T(8,128)(2,1)} %tok_hbm.1, bf16[128,4096]{1,0:T(8,128)(2,1)} %cot_hbm.1, s32[2,128]{1,0:T(2,128)} %bitcast.3, ...), custom_call_target="tpu_custom_call" | custom-call | tf_op jit(solution)/shard_map/experts/pallas_call | solution.py:485
  200.9 3.5 %hand_over.1 = (bf16[128,4096]{1,0:T(8,128)(2,1)}, bf16[128,4096]{1,0:T(8,128)(2,1)}, f32[2,128]{1,0:T(2,128)}, bf16[512,1536]{1,0:T(8,128)(2,1)}, bf16[96,4096]{1,0:T(8,128)(2,1)}) custom-call(bf16[128,4096]{1,0:T(8,128)(2,1)} %get-tuple-element.15.refs_0_, bf16[128,4096]{1,0:T(8,128)(2,1)} %get-tuple-element.16.refs_1_, ...), custom_call_target="tpu_custom_call" | custom-call | tf_op jit(solution)/shard_map/hand_over/pallas_call | solution.py:540

commit v5 on v4

--- a/solution.py
+++ b/solution.py
@@ -16,7 +16,7 @@
 ROWS = SLOTS * CAP
 TOK = 128
 OWN = 6
-PIECES = ((2, 0, 1024), (1, 0, 1024), (3, 0, 1024), (0, 0, 1024))
+PIECES = ((2, 0, 1024), (1, 0, 1024), (3, 0, 1024), (0, 0, 512), (0, 512, 512))
 QD = D // 4
 HD = D // 2
 

time: 205 us -> 204 us (level)
  no operation moved by 1% of the time
where the time goes in v5:
time: 204 us
  Pallas kernels  203 us (100%)
    pallas_call x1, Pallas kernels, shards(): pl.pallas_call(kernel, name='experts', out_shape=(jax.ShapeDtypeStruct((T...  200 us

profile of v5, /device:TPU:1, one launch (start us, length us, event | category | flops | bytes accessed | tf_op | source)
XLA Modules:
  0.0 204.0 jit_solution(9351213026096410660)
XLA Ops:
  0.6 199.6 %experts.1 = (bf16[128,4096]{1,0:T(8,128)(2,1)}, bf16[128,4096]{1,0:T(8,128)(2,1)}, f32[2,128]{1,0:T(2,128)}, bf16[512,1536]{1,0:T(8,128)(2,1)}, bf16[96,4096]{1,0:T(8,128)(2,1)}, /*index=5*/bf16[1536,2048]{1,0:T(8,128)(2,1)}) custom-call(bf16[128,4096]{1,0:T(8,128)(2,1)} %tok_hbm.1, bf16[128,4096]{1,0:T(8,128)(2,1)} %cot_hbm.1, s32[2,128]{1,0:T(2,128)} %bitcast.3, ...), custom_call_target="tpu_custom_call" | custom-call | tf_op jit(solution)/shard_map/experts/pallas_call | solution.py:485
  200.3 3.5 %hand_over.1 = (bf16[128,4096]{1,0:T(8,128)(2,1)}, bf16[128,4096]{1,0:T(8,128)(2,1)}, f32[2,128]{1,0:T(2,128)}, bf16[512,1536]{1,0:T(8,128)(2,1)}, bf16[96,4096]{1,0:T(8,128)(2,1)}) custom-call(bf16[128,4096]{1,0:T(8,128)(2,1)} %get-tuple-element.15.refs_0_, bf16[128,4096]{1,0:T(8,128)(2,1)} %get-tuple-element.16.refs_1_, ...), custom_call_target="tpu_custom_call" | custom-call | tf_op jit(solution)/shard_map/hand_over/pallas_call | solution.py:540
